TPU v7x, 32 devices: a whole 2x2x4 slice. The times are simulated.
32 devices in a mesh: lat: 4 (over y, x), lon: 8 (over z, core).
Axes of the slice: x: 2, y: 2, z: 4, core: 2. Of those that a mesh axis runs over, the one named last changes fastest.
Arguments:
- queries: bfloat16 [8, 32, 32, 640], P(None, 'lat', 'lon'), may hold values from -12 to 12
- key_vectors: bfloat16 [8, 32, 32, 640], P(None, 'lat', 'lon'), may hold values from -12 to 12
- values: bfloat16 [8, 32, 32, 640], P(None, 'lat', 'lon'), may hold values from -6 to 6
- upstream: bfloat16 [8, 32, 32, 640], P(None, 'lat', 'lon'), may hold values from -6 to 6
Outputs:
- attended: bfloat16 [8, 32, 32, 640], P(None, 'lat', 'lon')
- grad_queries: bfloat16 [8, 32, 32, 640], P(None, 'lat', 'lon')
- grad_keys: bfloat16 [8, 32, 32, 640], P(None, 'lat', 'lon')
- grad_values: bfloat16 [8, 32, 32, 640], P(None, 'lat', 'lon')
All inputs are finite; a program needn't handle non-finite values.
Results may differ from a plain program's by a relative error of at most 0.0044.
The roundings to bfloat16 on the way count: a program that leaves them out, or rounds other values in their place, can miss the bound.
Values may be sent and summed in bfloat16 or wider, within the bound.
A program may use at most 64 MiB of HBM per device.

v0:
```python
import jax
import jax.numpy as jnp
from jax import lax
from jax.sharding import PartitionSpec as P

HEAD_DIM = 64


def split_heads(tensor):
    leading = tensor.shape[0] * tensor.shape[1]
    return tensor.reshape(leading, tensor.shape[2], tensor.shape[3] // HEAD_DIM, HEAD_DIM)


def merge_heads(tensor, like):
    return tensor.astype(jnp.bfloat16).reshape(like.shape)


def softmax_weights(query_heads, key_heads):
    scores = jnp.einsum(
        "nqhd,nkhd->nhqk", query_heads, key_heads, preferred_element_type=jnp.float32
    ) * HEAD_DIM ** (-0.5)
    return jax.nn.softmax(scores, axis=-1)


def gradient_terms(query_heads, key_heads, value_heads, grad_heads):
    score_scale = HEAD_DIM ** (-0.5)
    probs = softmax_weights(query_heads, key_heads)
    rounded = probs.astype(jnp.bfloat16)
    grad_probs = jnp.einsum(
        "nqhd,nkhd->nhqk", grad_heads, value_heads, preferred_element_type=jnp.float32
    )
    row_delta = jnp.sum(probs * grad_probs, axis=-1, keepdims=True)
    grad_scores = (probs * (grad_probs - row_delta)).astype(jnp.bfloat16)
    grad_value_heads = jnp.einsum(
        "nhqk,nqhd->nkhd", rounded, grad_heads, preferred_element_type=jnp.float32
    )
    grad_query_heads = (
        jnp.einsum("nhqk,nkhd->nqhd", grad_scores, key_heads, preferred_element_type=jnp.float32)
        * score_scale
    )
    grad_key_heads = (
        jnp.einsum("nhqk,nqhd->nkhd", grad_scores, query_heads, preferred_element_type=jnp.float32)
        * score_scale
    )
    return (rounded, grad_query_heads, grad_key_heads, grad_value_heads)


def forward_local(inputs):
    queries, key_vectors, values = inputs
    probs = softmax_weights(split_heads(queries), split_heads(key_vectors))
    output = jnp.einsum(
        "nhqk,nkhd->nqhd",
        probs.astype(jnp.bfloat16),
        split_heads(values),
        preferred_element_type=jnp.float32,
    )
    return merge_heads(output, queries)


def backward_local(inputs):
    queries, key_vectors, values, upstream = inputs
    rounded, grad_q, grad_k, grad_v = gradient_terms(
        split_heads(queries), split_heads(key_vectors), split_heads(values), split_heads(upstream)
    )
    return (
        merge_heads(grad_q, queries),
        merge_heads(grad_k, queries),
        merge_heads(grad_v, queries),
    )


def lon_layout(tensor, groups):
    batch, rows, cols, feats = tensor.shape
    return tensor.reshape(groups, batch * rows // groups, cols, feats)


def lat_layout(tensor, groups):
    batch, rows, cols, feats = tensor.shape
    return tensor.transpose(0, 2, 1, 3).reshape(groups, batch * cols // groups, rows, feats)


def lon_restore(tensor, full_shape):
    return tensor.reshape(full_shape)


def lat_restore(tensor, full_shape):
    batch, rows, cols, feats = full_shape
    return tensor.reshape(batch, cols, rows, feats).transpose(0, 2, 1, 3)


def on_device(queries, key_vectors, values, upstream):
    full_shape = queries.shape
    lon_groups = lax.axis_size("lon")
    lat_groups = lax.axis_size("lat")
    inputs = (queries, key_vectors, values, upstream)
    lon_items = tuple((lon_layout(item, lon_groups) for item in inputs))
    lat_items = tuple((lat_layout(item, lat_groups) for item in inputs))
    lon_output = forward_local(
        (
            lax.all_to_all(lon_items[0], "lon", split_axis=0, concat_axis=2, tiled=True),
            lax.all_to_all(lon_items[1], "lon", split_axis=0, concat_axis=2, tiled=True),
            lax.all_to_all(lon_items[2], "lon", split_axis=0, concat_axis=2, tiled=True),
        )
    )
    lon_output = lax.all_to_all(lon_output, "lon", split_axis=2, concat_axis=0, tiled=True)
    lat_output = forward_local(
        (
            lax.all_to_all(lat_items[0], "lat", split_axis=0, concat_axis=2, tiled=True),
            lax.all_to_all(lat_items[1], "lat", split_axis=0, concat_axis=2, tiled=True),
            lax.all_to_all(lat_items[2], "lat", split_axis=0, concat_axis=2, tiled=True),
        )
    )
    lat_output = lax.all_to_all(lat_output, "lat", split_axis=2, concat_axis=0, tiled=True)
    lon_grads = backward_local(
        (
            lax.all_to_all(lon_items[0], "lon", split_axis=0, concat_axis=2, tiled=True),
            lax.all_to_all(lon_items[1], "lon", split_axis=0, concat_axis=2, tiled=True),
            lax.all_to_all(lon_items[2], "lon", split_axis=0, concat_axis=2, tiled=True),
            lax.all_to_all(lon_items[3], "lon", split_axis=0, concat_axis=2, tiled=True),
        )
    )
    lon_grads = (
        lax.all_to_all(lon_grads[0], "lon", split_axis=2, concat_axis=0, tiled=True),
        lax.all_to_all(lon_grads[1], "lon", split_axis=2, concat_axis=0, tiled=True),
        lax.all_to_all(lon_grads[2], "lon", split_axis=2, concat_axis=0, tiled=True),
    )
    lat_grads = backward_local(
        (
            lax.all_to_all(lat_items[0], "lat", split_axis=0, concat_axis=2, tiled=True),
            lax.all_to_all(lat_items[1], "lat", split_axis=0, concat_axis=2, tiled=True),
            lax.all_to_all(lat_items[2], "lat", split_axis=0, concat_axis=2, tiled=True),
            lax.all_to_all(lat_items[3], "lat", split_axis=0, concat_axis=2, tiled=True),
        )
    )
    lat_grads = (
        lax.all_to_all(lat_grads[0], "lat", split_axis=2, concat_axis=0, tiled=True),
        lax.all_to_all(lat_grads[1], "lat", split_axis=2, concat_axis=0, tiled=True),
        lax.all_to_all(lat_grads[2], "lat", split_axis=2, concat_axis=0, tiled=True),
    )
    lon_back = (lon_output, lon_grads[0], lon_grads[1], lon_grads[2])
    lat_back = (lat_output, lat_grads[0], lat_grads[1], lat_grads[2])
    results = []
    for lon_part, lat_part in zip(lon_back, lat_back):
        summed = lon_restore(lon_part, full_shape).astype(jnp.float32) + lat_restore(
            lat_part, full_shape
        ).astype(jnp.float32)
        results.append(summed.astype(jnp.bfloat16))
    return (results[0], results[1], results[2], results[3])


def solution(mesh):
    return jax.shard_map(
        on_device,
        mesh=mesh,
        in_specs=(
            P(None, "lat", "lon", None),
            P(None, "lat", "lon", None),
            P(None, "lat", "lon", None),
            P(None, "lat", "lon", None),
        ),
        out_specs=(
            P(None, "lat", "lon", None),
            P(None, "lat", "lon", None),
            P(None, "lat", "lon", None),
            P(None, "lat", "lon", None),
        ),
        check_vma=False,
    )
```

profile of v0, /device:TPU:0, one launch (start us, length us, event | category | flops | bytes accessed | tf_op | source)
XLA Modules:
  0.0 200.7 jit_solution(11766468155382825269)
XLA Ops:
  0.6 1.8 copy.130
  2.4 5.2 %all-to-all-start.4 = ((bf16[4,8,8,640]{3,2,1,0:T(8,128)(2,1)}), bf16[4,8,8,640]{3,2,1,0:T(8,128)(2,1)S(1)}, u32[]{:S(2)}, u32[]{:S(2)}) async-start(bf16[4,8,8,640]{3,2,1,0:T(8,128)(2,1)} %bitcast.12), calls=%async_computation.4 | async-start | bytes 655360 | tf_op jit(solution)/shard_map/all_to_all | solution.py:108
  7.6 1.7 copy.132
  9.3 4.2 %all-to-all-done.4 = bf16[4,8,8,640]{3,2,1,0:T(8,128)(2,1)S(1)} async-done(((bf16[4,8,8,640]{3,2,1,0:T(8,128)(2,1)}), bf16[4,8,8,640]{3,2,1,0:T(8,128)(2,1)S(1)}, u32[]{:S(2)}, u32[]{:S(2)}) %all-to-all-start.4) | async-done | bytes 327712 | tf_op jit(solution)/shard_map/all_to_all | solution.py:108
  13.5 3.5 %all-to-all-start.5 = ((bf16[4,8,8,640]{3,2,1,0:T(8,128)(2,1)}), bf16[4,8,8,640]{3,2,1,0:T(8,128)(2,1)S(1)}, u32[]{:S(2)}, u32[]{:S(2)}) async-start(bf16[4,8,8,640]{3,2,1,0:T(8,128)(2,1)} %bitcast.16), calls=%async_computation.5 | async-start | bytes 655360 | tf_op jit(solution)/shard_map/all_to_all | solution.py:109
  17.7 4.7 %all-to-all-done.5 = bf16[4,8,8,640]{3,2,1,0:T(8,128)(2,1)S(1)} async-done(((bf16[4,8,8,640]{3,2,1,0:T(8,128)(2,1)}), bf16[4,8,8,640]{3,2,1,0:T(8,128)(2,1)S(1)}, u32[]{:S(2)}, u32[]{:S(2)}) %all-to-all-start.5) | async-done | bytes 327712 | tf_op jit(solution)/shard_map/all_to_all | solution.py:109
  22.5 3.5 %all-to-all-start.6 = ((bf16[4,8,8,640]{3,2,1,0:T(8,128)(2,1)}), bf16[4,8,8,640]{3,2,1,0:T(8,128)(2,1)S(1)}, u32[]{:S(2)}, u32[]{:S(2)}) async-start(bf16[4,8,8,640]{3,2,1,0:T(8,128)(2,1)} %bitcast.20), calls=%async_computation.6 | async-start | bytes 655360 | tf_op jit(solution)/shard_map/all_to_all | solution.py:110
  26.9 4.5 %all-to-all-done.6 = bf16[4,8,8,640]{3,2,1,0:T(8,128)(2,1)S(1)} async-done(((bf16[4,8,8,640]{3,2,1,0:T(8,128)(2,1)}), bf16[4,8,8,640]{3,2,1,0:T(8,128)(2,1)S(1)}, u32[]{:S(2)}, u32[]{:S(2)}) %all-to-all-start.6) | async-done | bytes 327712 | tf_op jit(solution)/shard_map/all_to_all | solution.py:110
  31.4 8.8 %all_to_all.222 = bf16[4,8,8,640]{3,2,1,0:T(8,128)(2,1)S(1)} all-to-all(bf16[4,8,8,640]{3,2,1,0:T(8,128)(2,1)S(1)} %bitcast.181), channel_id=1, replica_groups=mesh['lat'=4,'lon'=8] {'lat'}, dimensions={0} | all-to-all | bytes 655360 | tf_op jit(solution)/shard_map/all_to_all | solution.py:132
  40.2 4.9 %all-to-all-start = ((bf16[8,8,4,640]{3,2,1,0:T(4,128)(2,1)}), bf16[8,8,4,640]{3,2,1,0:T(4,128)(2,1)S(1)}, u32[]{:S(2)}, u32[]{:S(2)}) async-start(bf16[8,8,4,640]{3,2,1,0:T(4,128)(2,1)} %param.4), calls=%async_computation | async-start | bytes 655360 | tf_op jit(solution)/shard_map/all_to_all | solution.py:100
  45.2 1.5 reshape.142
  46.7 1.5 reshape.137
  49.4 6.8 %all-to-all-done = bf16[8,8,4,640]{3,2,1,0:T(4,128)(2,1)S(1)} async-done(((bf16[8,8,4,640]{3,2,1,0:T(4,128)(2,1)}), bf16[8,8,4,640]{3,2,1,0:T(4,128)(2,1)S(1)}, u32[]{:S(2)}, u32[]{:S(2)}) %all-to-all-start) | async-done | bytes 327712 | tf_op jit(solution)/shard_map/all_to_all | solution.py:100
  56.9 4.1 %all-to-all-start.1 = ((bf16[8,8,4,640]{3,2,1,0:T(4,128)(2,1)}), bf16[8,8,4,640]{3,2,1,0:T(4,128)(2,1)}, u32[]{:S(2)}, u32[]{:S(2)}) async-start(bf16[8,8,4,640]{3,2,1,0:T(4,128)(2,1)} %param.5), calls=%async_computation.1 | async-start | bytes 655360 | tf_op jit(solution)/shard_map/all_to_all | solution.py:101
  61.7 3.6 %multiply_reduce_fusion = (f32[8,10,32]{2,1,0:T(8,128)S(1)}, f32[8,10,32,32]{2,3,1,0:T(8,128)}) fusion(f32[8,10,32,32]{2,3,1,0:T(8,128)S(1)} %get-tuple-element.17, f32[8,10,32]{2,1,0:T(8,128)S(1)} %get-tuple-element.16, bf16[8,32,10,64]{3,2,1,0:T(8,128)(2,1)} %reshape.137, bf16[8,32,10,64]{3,2,1,0:T(8,128)(2,1)} %reshape.142), kind=kOutput, calls=%fused_computation.21 | convolution fusion | flops 10728960 | bytes 1331200 | tf_op jit(solution)/shard_map/nqhd,nkhd->nhqk/dot_general | solution.py:29
  65.3 6.8 %all-to-all-done.1 = bf16[8,8,4,640]{3,2,1,0:T(4,128)(2,1)} async-done(((bf16[8,8,4,640]{3,2,1,0:T(4,128)(2,1)}), bf16[8,8,4,640]{3,2,1,0:T(4,128)(2,1)}, u32[]{:S(2)}, u32[]{:S(2)}) %all-to-all-start.1) | async-done | bytes 327712 | tf_op jit(solution)/shard_map/all_to_all | solution.py:101
  72.2 4.1 %all-to-all-start.2 = ((bf16[8,8,4,640]{3,2,1,0:T(4,128)(2,1)}), bf16[8,8,4,640]{3,2,1,0:T(4,128)(2,1)}, u32[]{:S(2)}, u32[]{:S(2)}) async-start(bf16[8,8,4,640]{3,2,1,0:T(4,128)(2,1)} %param.6), calls=%async_computation.2 | async-start | bytes 655360 | tf_op jit(solution)/shard_map/all_to_all | solution.py:102
  76.3 2.1 %multiply_convert_fusion = bf16[8,10,32,32]{2,3,1,0:T(8,128)(2,1)S(1)} fusion(f32[8,10,32,32]{2,3,1,0:T(8,128)} %get-tuple-element.21, f32[8,10,32]{2,1,0:T(8,128)S(1)} %get-tuple-element.20, f32[8,10,32,32]{2,3,1,0:T(8,128)} %copy-done.4, f32[8,10,32]{2,1,0:T(8,128)S(1)} %get-tuple-element.16), kind=kLoop, calls=%fused_computation.20 | loop fusion | flops 327680 | bytes 839680 | tf_op jit(solution)/shard_map/convert_element_type | solution.py:33
  79.1 1.3 reshape.167
  82.4 5.0 %all-to-all-done.2 = bf16[8,8,4,640]{3,2,1,0:T(4,128)(2,1)} async-done(((bf16[8,8,4,640]{3,2,1,0:T(4,128)(2,1)}), bf16[8,8,4,640]{3,2,1,0:T(4,128)(2,1)}, u32[]{:S(2)}, u32[]{:S(2)}) %all-to-all-start.2) | async-done | bytes 327712 | tf_op jit(solution)/shard_map/all_to_all | solution.py:102
  87.4 3.4 %all-to-all-start.8 = ((bf16[8,8,4,640]{3,2,1,0:T(4,128)(2,1)}), bf16[8,8,4,640]{3,2,1,0:T(4,128)(2,1)S(1)}, u32[]{:S(2)}, u32[]{:S(2)}) async-start(bf16[8,8,4,640]{3,2,1,0:T(4,128)(2,1)} %param.7), calls=%async_computation.8 | async-start | bytes 655360 | tf_op jit(solution)/shard_map/all_to_all | solution.py:119
  90.8 1.6 fusion.11
  92.8 1.3 reshape.165
  94.1 1.5 fusion.13
  96.0 1.3 reshape.171
  99.4 2.5 %all-to-all-done.8 = bf16[8,8,4,640]{3,2,1,0:T(4,128)(2,1)S(1)} async-done(((bf16[8,8,4,640]{3,2,1,0:T(4,128)(2,1)}), bf16[8,8,4,640]{3,2,1,0:T(4,128)(2,1)S(1)}, u32[]{:S(2)}, u32[]{:S(2)}) %all-to-all-start.8) | async-done | bytes 327712 | tf_op jit(solution)/shard_map/all_to_all | solution.py:119
  101.9 4.3 %all-to-all-start.11 = ((bf16[1,8,32,640]{3,1,0,2:T(8,128)(2,1)}), bf16[1,8,32,640]{3,1,0,2:T(8,128)(2,1)}, u32[]{:S(2)}, u32[]{:S(2)}) async-start(bf16[1,8,32,640]{3,1,0,2:T(8,128)(2,1)} %reshape.167), calls=%async_computation.11 | async-start | bytes 655360 | tf_op jit(solution)/shard_map/all_to_all | solution.py:136
  106.3 1.5 reshape.139
  107.8 1.5 reshape.130
  111.8 4.1 %all-to-all-start.13 = ((bf16[1,8,32,640]{3,1,0,2:T(8,128)(2,1)}), bf16[1,8,32,640]{3,1,0,2:T(8,128)(2,1)}, u32[]{:S(2)}, u32[]{:S(2)}) async-start(bf16[1,8,32,640]{3,1,0,2:T(8,128)(2,1)} %reshape.169), calls=%async_computation.13 | async-start | bytes 655360 | tf_op jit(solution)/shard_map/all_to_all | solution.py:137
  115.9 3.7 %multiply_reduce_fusion.1 = (f32[8,10,32]{2,1,0:T(8,128)S(1)}, f32[8,10,32,32]{2,3,1,0:T(8,128)}) fusion(f32[8,10,32,32]{2,3,1,0:T(8,128)S(1)} %get-tuple-element.19, f32[8,10,32]{2,1,0:T(8,128)S(1)} %get-tuple-element.18, bf16[8,32,10,64]{3,2,0,1:T(8,128)(2,1)} %reshape.130, bf16[8,32,10,64]{3,2,0,1:T(8,128)(2,1)} %reshape.139), kind=kOutput, calls=%fused_computation.23 | convolution fusion | flops 10728960 | bytes 1331200 | tf_op jit(solution)/shard_map/nqhd,nkhd->nhqk/dot_general | solution.py:29
  119.6 1.9 all-to-all-done.13
  121.5 4.1 %all-to-all-start.7 = ((bf16[1,8,32,640]{3,1,0,2:T(8,128)(2,1)}), bf16[1,8,32,640]{3,1,0,2:T(8,128)(2,1)}, u32[]{:S(2)}, u32[]{:S(2)}) async-start(bf16[1,8,32,640]{3,1,0,2:T(8,128)(2,1)} %reshape.165), calls=%async_computation.7 | async-start | bytes 655360 | tf_op jit(solution)/shard_map/all_to_all | solution.py:113
  125.7 2.1 %multiply_convert_fusion.1 = bf16[8,10,32,32]{2,3,1,0:T(8,128)(2,1)S(1)} fusion(f32[8,10,32,32]{2,3,1,0:T(8,128)} %get-tuple-element.23, f32[8,10,32]{2,1,0:T(8,128)S(1)} %get-tuple-element.22, f32[8,10,32,32]{2,3,1,0:T(8,128)} %copy-done.2, f32[8,10,32]{2,1,0:T(8,128)S(1)} %get-tuple-element.18), kind=kLoop, calls=%fused_computation.22 | loop fusion | flops 327680 | bytes 839680 | tf_op jit(solution)/shard_map/convert_element_type | solution.py:33
  127.8 3.5 %all-to-all-done.7 = bf16[1,8,32,640]{3,1,0,2:T(8,128)(2,1)} async-done(((bf16[1,8,32,640]{3,1,0,2:T(8,128)(2,1)}), bf16[1,8,32,640]{3,1,0,2:T(8,128)(2,1)}, u32[]{:S(2)}, u32[]{:S(2)}) %all-to-all-start.7) | async-done | bytes 327712 | tf_op jit(solution)/shard_map/all_to_all | solution.py:113
  131.3 3.5 %all-to-all-start.15 = ((bf16[1,8,32,640]{3,1,0,2:T(8,128)(2,1)}), bf16[1,8,32,640]{3,1,0,2:T(8,128)(2,1)S(1)}, u32[]{:S(2)}, u32[]{:S(2)}) async-start(bf16[1,8,32,640]{3,1,0,2:T(8,128)(2,1)} %reshape.171), calls=%async_computation.15 | async-start | bytes 655360 | tf_op jit(solution)/shard_map/all_to_all | solution.py:138
  135.7 1.3 reshape.166
  137.0 3.3 %all-to-all-done.15 = bf16[1,8,32,640]{3,1,0,2:T(8,128)(2,1)S(1)} async-done(((bf16[1,8,32,640]{3,1,0,2:T(8,128)(2,1)}), bf16[1,8,32,640]{3,1,0,2:T(8,128)(2,1)S(1)}, u32[]{:S(2)}, u32[]{:S(2)}) %all-to-all-start.15) | async-done | bytes 327712 | tf_op jit(solution)/shard_map/all_to_all | solution.py:138
  141.0 3.4 %all-to-all-start.9 = ((bf16[1,8,32,640]{3,1,0,2:T(8,128)(2,1)}), bf16[1,8,32,640]{3,1,0,2:T(8,128)(2,1)S(1)}, u32[]{:S(2)}, u32[]{:S(2)}) async-start(bf16[1,8,32,640]{3,1,0,2:T(8,128)(2,1)} %reshape.166), calls=%async_computation.9 | async-start | bytes 655360 | tf_op jit(solution)/shard_map/all_to_all | solution.py:123
  145.3 1.3 reshape.168
  146.6 9.0 %all-to-all-done.9 = bf16[1,8,32,640]{3,1,0,2:T(8,128)(2,1)S(1)} async-done(((bf16[1,8,32,640]{3,1,0,2:T(8,128)(2,1)}), bf16[1,8,32,640]{3,1,0,2:T(8,128)(2,1)S(1)}, u32[]{:S(2)}, u32[]{:S(2)}) %all-to-all-start.9) | async-done | bytes 327712 | tf_op jit(solution)/shard_map/all_to_all | solution.py:123
  155.5 3.4 %all-to-all-start.12 = ((bf16[1,8,32,640]{3,1,0,2:T(8,128)(2,1)}), bf16[1,8,32,640]{3,1,0,2:T(8,128)(2,1)S(1)}, u32[]{:S(2)}, u32[]{:S(2)}) async-start(bf16[1,8,32,640]{3,1,0,2:T(8,128)(2,1)} %reshape.168), calls=%async_computation.12 | async-start | bytes 655360 | tf_op jit(solution)/shard_map/all_to_all | solution.py:124
  161.0 1.9 fusion.10
  164.6 5.4 %all-to-all-done.12 = bf16[1,8,32,640]{3,1,0,2:T(8,128)(2,1)S(1)} async-done(((bf16[1,8,32,640]{3,1,0,2:T(8,128)(2,1)}), bf16[1,8,32,640]{3,1,0,2:T(8,128)(2,1)S(1)}, u32[]{:S(2)}, u32[]{:S(2)}) %all-to-all-start.12) | async-done | bytes 327712 | tf_op jit(solution)/shard_map/all_to_all | solution.py:124
  170.1 4.3 %all-to-all-start.3 = ((bf16[1,8,32,640]{3,1,0,2:T(8,128)(2,1)}), bf16[1,8,32,640]{3,1,0,2:T(8,128)(2,1)}, u32[]{:S(2)}, u32[]{:S(2)}) async-start(bf16[1,8,32,640]{3,1,0,2:T(8,128)(2,1)} %reshape.164), calls=%async_computation.3 | async-start | bytes 655360 | tf_op jit(solution)/shard_map/all_to_all | solution.py:105
  180.9 4.4 %all-to-all-done.3 = bf16[1,8,32,640]{3,1,0,2:T(8,128)(2,1)} async-done(((bf16[1,8,32,640]{3,1,0,2:T(8,128)(2,1)}), bf16[1,8,32,640]{3,1,0,2:T(8,128)(2,1)}, u32[]{:S(2)}, u32[]{:S(2)}) %all-to-all-start.3) | async-done | bytes 327712 | tf_op jit(solution)/shard_map/all_to_all | solution.py:105
  185.3 3.4 %all-to-all-start.14 = ((bf16[1,8,32,640]{3,1,0,2:T(8,128)(2,1)}), bf16[1,8,32,640]{3,1,0,2:T(8,128)(2,1)S(1)}, u32[]{:S(2)}, u32[]{:S(2)}) async-start(bf16[1,8,32,640]{3,1,0,2:T(8,128)(2,1)} %reshape.170), calls=%async_computation.14 | async-start | bytes 655360 | tf_op jit(solution)/shard_map/all_to_all | solution.py:125
  193.5 6.3 %all-to-all-done.14 = bf16[1,8,32,640]{3,1,0,2:T(8,128)(2,1)S(1)} async-done(((bf16[1,8,32,640]{3,1,0,2:T(8,128)(2,1)}), bf16[1,8,32,640]{3,1,0,2:T(8,128)(2,1)S(1)}, u32[]{:S(2)}, u32[]{:S(2)}) %all-to-all-start.14) | async-done | bytes 327712 | tf_op jit(solution)/shard_map/all_to_all | solution.py:125
  (75 shorter events, 30.8 us)
Async XLA Ops:
  0.6 16.3 %copy-start.6 = (bf16[8,8,4,640]{3,2,1,0:T(4,128)(2,1)S(1)}, bf16[8,8,4,640]{3,2,1,0:T(4,128)(2,1)}, u32[]{:S(2)}) copy-start(bf16[8,8,4,640]{3,2,1,0:T(4,128)(2,1)} %param.6) | copy-start | bytes 983044
  2.4 11.1 %all-to-all-start.4 = ((bf16[4,8,8,640]{3,2,1,0:T(8,128)(2,1)}), bf16[4,8,8,640]{3,2,1,0:T(8,128)(2,1)S(1)}, u32[]{:S(2)}, u32[]{:S(2)}) async-start(bf16[4,8,8,640]{3,2,1,0:T(8,128)(2,1)} %bitcast.12), calls=%async_computation.4 | async-start | bytes 655360 | tf_op jit(solution)/shard_map/all_to_all | solution.py:108
  13.5 9.0 %all-to-all-start.5 = ((bf16[4,8,8,640]{3,2,1,0:T(8,128)(2,1)}), bf16[4,8,8,640]{3,2,1,0:T(8,128)(2,1)S(1)}, u32[]{:S(2)}, u32[]{:S(2)}) async-start(bf16[4,8,8,640]{3,2,1,0:T(8,128)(2,1)} %bitcast.16), calls=%async_computation.5 | async-start | bytes 655360 | tf_op jit(solution)/shard_map/all_to_all | solution.py:109
  22.5 9.0 %all-to-all-start.6 = ((bf16[4,8,8,640]{3,2,1,0:T(8,128)(2,1)}), bf16[4,8,8,640]{3,2,1,0:T(8,128)(2,1)S(1)}, u32[]{:S(2)}, u32[]{:S(2)}) async-start(bf16[4,8,8,640]{3,2,1,0:T(8,128)(2,1)} %bitcast.20), calls=%async_computation.6 | async-start | bytes 655360 | tf_op jit(solution)/shard_map/all_to_all | solution.py:110
  40.2 16.0 %all-to-all-start = ((bf16[8,8,4,640]{3,2,1,0:T(4,128)(2,1)}), bf16[8,8,4,640]{3,2,1,0:T(4,128)(2,1)S(1)}, u32[]{:S(2)}, u32[]{:S(2)}) async-start(bf16[8,8,4,640]{3,2,1,0:T(4,128)(2,1)} %param.4), calls=%async_computation | async-start | bytes 655360 | tf_op jit(solution)/shard_map/all_to_all | solution.py:100
  56.2 0.7 copy-start.7
  56.9 15.2 %all-to-all-start.1 = ((bf16[8,8,4,640]{3,2,1,0:T(4,128)(2,1)}), bf16[8,8,4,640]{3,2,1,0:T(4,128)(2,1)}, u32[]{:S(2)}, u32[]{:S(2)}) async-start(bf16[8,8,4,640]{3,2,1,0:T(4,128)(2,1)} %param.5), calls=%async_computation.1 | async-start | bytes 655360 | tf_op jit(solution)/shard_map/all_to_all | solution.py:101
  61.7 14.5 %copy-start.4 = (f32[8,10,32,32]{2,3,1,0:T(8,128)}, f32[8,10,32,32]{2,3,1,0:T(8,128)S(1)}, u32[]{:S(2)}) copy-start(f32[8,10,32,32]{2,3,1,0:T(8,128)S(1)} %get-tuple-element.17) | copy-start | bytes 983044
  72.2 15.2 %all-to-all-start.2 = ((bf16[8,8,4,640]{3,2,1,0:T(4,128)(2,1)}), bf16[8,8,4,640]{3,2,1,0:T(4,128)(2,1)}, u32[]{:S(2)}, u32[]{:S(2)}) async-start(bf16[8,8,4,640]{3,2,1,0:T(4,128)(2,1)} %param.6), calls=%async_computation.2 | async-start | bytes 655360 | tf_op jit(solution)/shard_map/all_to_all | solution.py:102
  81.1 9.8 %copy-start.5 = (f32[8,10,32,32]{2,3,1,0:T(8,128)S(1)}, f32[8,10,32,32]{2,3,1,0:T(8,128)}, u32[]{:S(2)}) copy-start(f32[8,10,32,32]{2,3,1,0:T(8,128)} %copy-done.4) | copy-start | bytes 983044
  87.4 14.5 %all-to-all-start.8 = ((bf16[8,8,4,640]{3,2,1,0:T(4,128)(2,1)}), bf16[8,8,4,640]{3,2,1,0:T(4,128)(2,1)S(1)}, u32[]{:S(2)}, u32[]{:S(2)}) async-start(bf16[8,8,4,640]{3,2,1,0:T(4,128)(2,1)} %param.7), calls=%async_computation.8 | async-start | bytes 655360 | tf_op jit(solution)/shard_map/all_to_all | solution.py:119
  95.7 1.7 copy-start.8
  101.9 9.9 %all-to-all-start.11 = ((bf16[1,8,32,640]{3,1,0,2:T(8,128)(2,1)}), bf16[1,8,32,640]{3,1,0,2:T(8,128)(2,1)}, u32[]{:S(2)}, u32[]{:S(2)}) async-start(bf16[1,8,32,640]{3,1,0,2:T(8,128)(2,1)} %reshape.167), calls=%async_computation.11 | async-start | bytes 655360 | tf_op jit(solution)/shard_map/all_to_all | solution.py:136
  111.6 9.9 %copy-start.2 = (f32[8,10,32,32]{2,3,1,0:T(8,128)}, f32[8,10,32,32]{2,3,1,0:T(8,128)S(1)}, u32[]{:S(2)}) copy-start(f32[8,10,32,32]{2,3,1,0:T(8,128)S(1)} %get-tuple-element.19) | copy-start | bytes 983044
  111.8 9.7 %all-to-all-start.13 = ((bf16[1,8,32,640]{3,1,0,2:T(8,128)(2,1)}), bf16[1,8,32,640]{3,1,0,2:T(8,128)(2,1)}, u32[]{:S(2)}, u32[]{:S(2)}) async-start(bf16[1,8,32,640]{3,1,0,2:T(8,128)(2,1)} %reshape.169), calls=%async_computation.13 | async-start | bytes 655360 | tf_op jit(solution)/shard_map/all_to_all | solution.py:137
  121.5 9.7 %all-to-all-start.7 = ((bf16[1,8,32,640]{3,1,0,2:T(8,128)(2,1)}), bf16[1,8,32,640]{3,1,0,2:T(8,128)(2,1)}, u32[]{:S(2)}, u32[]{:S(2)}) async-start(bf16[1,8,32,640]{3,1,0,2:T(8,128)(2,1)} %reshape.165), calls=%async_computation.7 | async-start | bytes 655360 | tf_op jit(solution)/shard_map/all_to_all | solution.py:113
  131.3 9.0 %all-to-all-start.15 = ((bf16[1,8,32,640]{3,1,0,2:T(8,128)(2,1)}), bf16[1,8,32,640]{3,1,0,2:T(8,128)(2,1)S(1)}, u32[]{:S(2)}, u32[]{:S(2)}) async-start(bf16[1,8,32,640]{3,1,0,2:T(8,128)(2,1)} %reshape.171), calls=%async_computation.15 | async-start | bytes 655360 | tf_op jit(solution)/shard_map/all_to_all | solution.py:138
  140.2 0.7 copy-start.9
  141.0 14.6 %all-to-all-start.9 = ((bf16[1,8,32,640]{3,1,0,2:T(8,128)(2,1)}), bf16[1,8,32,640]{3,1,0,2:T(8,128)(2,1)S(1)}, u32[]{:S(2)}, u32[]{:S(2)}) async-start(bf16[1,8,32,640]{3,1,0,2:T(8,128)(2,1)} %reshape.166), calls=%async_computation.9 | async-start | bytes 655360 | tf_op jit(solution)/shard_map/all_to_all | solution.py:123
  146.6 14.4 %copy-start.12 = (bf16[8,32,10,64]{3,2,0,1:T(8,128)(2,1)S(1)}, bf16[8,32,10,64]{3,2,0,1:T(8,128)(2,1)}, u32[]{:S(2)}) copy-start(bf16[8,32,10,64]{3,2,0,1:T(8,128)(2,1)} %reshape.130) | copy-start | bytes 983044
  155.5 14.5 %all-to-all-start.12 = ((bf16[1,8,32,640]{3,1,0,2:T(8,128)(2,1)}), bf16[1,8,32,640]{3,1,0,2:T(8,128)(2,1)S(1)}, u32[]{:S(2)}, u32[]{:S(2)}) async-start(bf16[1,8,32,640]{3,1,0,2:T(8,128)(2,1)} %reshape.168), calls=%async_computation.12 | async-start | bytes 655360 | tf_op jit(solution)/shard_map/all_to_all | solution.py:124
  170.0 6.2 %copy-start = (bf16[1,8,32,640]{3,1,0,2:T(8,128)(2,1)}, bf16[1,8,32,640]{3,1,0,2:T(8,128)(2,1)S(1)}, u32[]{:S(2)}) copy-start(bf16[1,8,32,640]{3,1,0,2:T(8,128)(2,1)S(1)} %all-to-all-done.12) | copy-start | bytes 983044
  170.1 15.2 %all-to-all-start.3 = ((bf16[1,8,32,640]{3,1,0,2:T(8,128)(2,1)}), bf16[1,8,32,640]{3,1,0,2:T(8,128)(2,1)}, u32[]{:S(2)}, u32[]{:S(2)}) async-start(bf16[1,8,32,640]{3,1,0,2:T(8,128)(2,1)} %reshape.164), calls=%async_computation.3 | async-start | bytes 655360 | tf_op jit(solution)/shard_map/all_to_all | solution.py:105
  176.3 1.0 copy-start.10
  176.3 1.3 copy-start.11
  177.3 1.4 copy-start.3
  180.9 9.8 %copy-start.1 = (bf16[1,8,32,640]{3,1,0,2:T(8,128)(2,1)S(1)}, bf16[1,8,32,640]{3,1,0,2:T(8,128)(2,1)}, u32[]{:S(2)}) copy-start(bf16[1,8,32,640]{3,1,0,2:T(8,128)(2,1)} %copy-done) | copy-start | bytes 983044
  185.3 14.5 %all-to-all-start.14 = ((bf16[1,8,32,640]{3,1,0,2:T(8,128)(2,1)}), bf16[1,8,32,640]{3,1,0,2:T(8,128)(2,1)S(1)}, u32[]{:S(2)}, u32[]{:S(2)}) async-start(bf16[1,8,32,640]{3,1,0,2:T(8,128)(2,1)} %reshape.170), calls=%async_computation.14 | async-start | bytes 655360 | tf_op jit(solution)/shard_map/all_to_all | solution.py:125
where the time goes:
time: 203 us; the launch traced here: 201 us
  waiting for transfers between devices  68.5 us (34%)
  starting transfers between devices  59.1 us (29%)
  local copies, waits for them, and re-layouts  37 us (18%)
  matrix products  16.7 us (8%)
  other arithmetic  9.6 us (5%)
  blocking collectives  8.75 us (4%)
    reshape x16, local copies, waits for them, and re-layouts, merge_heads(): return tensor.astype(jnp.bfloat16).reshape(like.shape)  13.1 us
    unnamed x34, local copies, waits for them, and re-layouts  12.3 us
    all_to_all x1, waiting for transfers between devices, on_device(): lax.all_to_all(lon_grads[0], 'lon', split_axis=2, concat_axis=0, tiled=True)  8.95 us
    all_to_all x1, blocking collectives, on_device(): lax.all_to_all(lat_items[3], 'lat', split_axis=0, concat_axis=2, tiled=True)  8.75 us
    reshape x8, local copies, waits for them, and re-layouts, split_heads(): tensor.reshape(leading, tensor.shape[2], tensor.shape[3] // HEAD_DIM, HEA...  8.33 us
    dot_general x2, matrix products, gradient_terms(): jnp.einsum('nqhd,nkhd->nhqk', grad_heads, value_heads, preferred_element_...  7.27 us
    all_to_all x1, waiting for transfers between devices, on_device(): lax.all_to_all(lon_items[1], 'lon', split_axis=0, concat_axis=2, tiled=True)  6.84 us
    all_to_all x1, waiting for transfers between devices, on_device(): lax.all_to_all(lon_items[0], 'lon', split_axis=0, concat_axis=2, tiled=True)  6.82 us
  transfers between devices with their start and end apart: 15, of which 15 were waited for; matrix products, arithmetic and copies ran while one was open for 28% of the time, Pallas kernels for 0%

commit v1 on v0

v1 whole, which is shorter than its diff:
```python
import functools

import jax
import jax.numpy as jnp
from jax import lax
from jax.experimental import pallas as pl
from jax.experimental.pallas import tpu as pltpu
from jax.sharding import PartitionSpec as P

HEAD_DIM = 64
LANES = 128
SUBROWS = 16
SCALE = HEAD_DIM ** (-0.5)
F32 = jnp.float32
BF16 = jnp.bfloat16


def contract(left, right, dims):
    return lax.dot_general(left, right, ((dims[:1], dims[1:]), ((), ())), preferred_element_type=F32)


def lines_block(q, k, v, g, same, low, high):
    tokens = q.shape[0]
    q2 = jnp.concatenate([q * low, q * high], axis=0)
    k2 = jnp.concatenate([k * low, k * high], axis=0)
    v2 = jnp.concatenate([v * low, v * high], axis=0)
    g2 = jnp.concatenate([g * low, g * high], axis=0)
    scores = contract(q, k2, (1, 1))
    gprobs = contract(g, v2, (1, 1))
    probs_b, gscores_b = [], []
    for head in range(2):
        cut = slice(head * tokens, (head + 1) * tokens)
        s = jnp.where(same, scores[:, cut] * SCALE, -1e30)
        e = jnp.exp(s - jnp.max(s, axis=1, keepdims=True))
        p = e / jnp.sum(e, axis=1, keepdims=True)
        d = gprobs[:, cut]
        delta = jnp.sum(p * d, axis=1, keepdims=True)
        probs_b.append(p.astype(BF16))
        gscores_b.append((p * (d - delta)).astype(BF16))
    out = contract(jnp.concatenate(probs_b, axis=1), v2, (1, 0))
    dq = contract(jnp.concatenate(gscores_b, axis=1), k2, (1, 0)) * SCALE
    dk = contract(jnp.concatenate(gscores_b, axis=0), q2, (0, 0)) * SCALE
    dv = contract(jnp.concatenate(probs_b, axis=0), g2, (0, 0))
    return out.astype(BF16), dq.astype(BF16), dk.astype(BF16), dv.astype(BF16)


def kernel(
    n_lat, n_lon, cols, x_ref, out_ref,
    in_lat, in_lon, res_lat, res_lon, ret_lat, ret_lon,
    s_in_lat, r_in_lat, s_in_lon, r_in_lon, s_out_lat, r_out_lat, s_out_lon, r_out_lon, own_sem,
):
    me_lat = lax.axis_index("lat")
    me_lon = lax.axis_index("lon")
    _, batch, tokens, feats = x_ref.shape
    per_lat = batch // n_lat
    parts = tokens // SUBROWS
    lat_peers = [(d, lax.rem(me_lat + d, n_lat)) for d in range(1, n_lat)]
    lon_order = sorted(range(1, n_lon), key=lambda d: abs(d - n_lon // 2))
    lon_peers = [(d, lax.rem(me_lon + d, n_lon)) for d in lon_order]

    barrier = pltpu.get_barrier_semaphore()
    for _, peer in lat_peers:
        pl.semaphore_signal(barrier, inc=1, device_id={"lat": peer}, device_id_type=pl.DeviceIdType.MESH)
    for _, peer in lon_peers:
        pl.semaphore_signal(barrier, inc=1, device_id={"lon": peer}, device_id_type=pl.DeviceIdType.MESH)
    pl.semaphore_wait(barrier, len(lat_peers) + len(lon_peers))

    def remote(src, dst, send, recv, target):
        return pltpu.make_async_remote_copy(
            src_ref=src, dst_ref=dst, send_sem=send, recv_sem=recv,
            device_id=target, device_id_type=pl.DeviceIdType.MESH,
        )

    def lat_in(i, d, peer):
        return remote(
            x_ref.at[:, peer * per_lat + i], in_lat.at[:, i, me_lat],
            s_in_lat.at[i, d], r_in_lat.at[i, d], {"lat": peer},
        )

    def lon_in(i, d, peer):
        return remote(
            x_ref.at[:, peer, pl.ds(i * SUBROWS, SUBROWS)], in_lon.at[:, i, me_lon],
            s_in_lon.at[i, d], r_in_lon.at[i, d], {"lon": peer},
        )

    def lat_out(i, d, peer):
        return remote(
            res_lat.at[:, i, peer], ret_lat.at[:, me_lat * per_lat + i],
            s_out_lat.at[i, d], r_out_lat.at[i, d], {"lat": peer},
        )

    def lon_out(i, d, peer):
        return remote(
            res_lon.at[:, i, peer], ret_lon.at[:, me_lon, pl.ds(i * SUBROWS, SUBROWS)],
            s_out_lon.at[i, d], r_out_lon.at[i, d], {"lon": peer},
        )

    for i in range(max(per_lat, parts)):
        if i < parts:
            for d, peer in lon_peers:
                lon_in(i, d, peer).start()
        if i < per_lat:
            for d, peer in lat_peers:
                lat_in(i, d, peer).start()

    owns = []
    for i in range(per_lat):
        owns.append(pltpu.make_async_copy(
            x_ref.at[:, me_lat * per_lat + i], in_lat.at[:, i, me_lat], own_sem.at[len(owns)]))
    for i in range(parts):
        owns.append(pltpu.make_async_copy(
            x_ref.at[:, me_lon, pl.ds(i * SUBROWS, SUBROWS)], in_lon.at[:, i, me_lon], own_sem.at[len(owns)]))
    for copy in owns:
        copy.start()

    lane = lax.broadcasted_iota(jnp.int32, (1, LANES), 1)
    low = (lane < HEAD_DIM).astype(F32).astype(BF16)
    high = (lane >= HEAD_DIM).astype(F32).astype(BF16)

    def attend(arrived, result, i, same):
        count, rows = arrived.shape[2], arrived.shape[3]

        def pair(h, carry):
            cut = pl.ds(pl.multiple_of(h * LANES, LANES), LANES)
            items = [arrived[a, i, :, :, cut].reshape(count * rows, LANES) for a in range(4)]
            for o, value in enumerate(lines_block(*items, same, low, high)):
                result[o, i, :, :, cut] = value.reshape(count, rows, LANES)
            return carry

        lax.fori_loop(0, feats // LANES, pair, 0)

    def same_line(size, line_of):
        a = line_of(lax.broadcasted_iota(jnp.int32, (size, size), 0))
        b = line_of(lax.broadcasted_iota(jnp.int32, (size, size), 1))
        return a == b

    same_lat = same_line(n_lat * tokens, lambda t: lax.rem(t, cols))
    same_lon = same_line(n_lon * SUBROWS, lambda t: lax.div(lax.rem(t, SUBROWS), cols))

    for i in range(per_lat):
        owns[i].wait()
        for d, peer in lat_peers:
            lat_in(i, d, peer).wait_recv()
        attend(in_lat, res_lat, i, same_lat)
        for d, peer in lat_peers:
            lat_out(i, d, peer).start()
        keep = pltpu.make_async_copy(
            res_lat.at[:, i, me_lat], ret_lat.at[:, me_lat * per_lat + i], own_sem.at[i])
        keep.start()
        owns[i] = keep
    for i in range(parts):
        owns[per_lat + i].wait()
        for d, peer in lon_peers:
            lon_in(i, d, peer).wait_recv()
        attend(in_lon, res_lon, i, same_lon)
        for d, peer in lon_peers:
            lon_out(i, d, peer).start()
        keep = pltpu.make_async_copy(
            res_lon.at[:, i, me_lon], ret_lon.at[:, me_lon, pl.ds(i * SUBROWS, SUBROWS)], own_sem.at[per_lat + i])
        keep.start()
        owns[per_lat + i] = keep

    for copy in owns:
        copy.wait()
    for i in range(per_lat):
        for d, peer in lat_peers:
            lat_out(i, d, peer).wait_recv()
    for i in range(parts):
        for d, peer in lon_peers:
            lon_out(i, d, peer).wait_recv()

        def add(b, carry):
            rows = pl.ds(i * SUBROWS, SUBROWS)
            for o in range(4):
                total = ret_lat[o, b, rows, :].astype(F32) + ret_lon[o, b, rows, :].astype(F32)
                out_ref[o, b, rows, :] = total.astype(BF16)
            return carry

        lax.fori_loop(0, batch, add, 0)

    for i in range(per_lat):
        for d, peer in lat_peers:
            lat_in(i, d, peer).wait_send()
            lat_out(i, d, peer).wait_send()
    for i in range(parts):
        for d, peer in lon_peers:
            lon_in(i, d, peer).wait_send()
            lon_out(i, d, peer).wait_send()


def by_kernel(n_lat, n_lon, queries, key_vectors, values, upstream):
    batch, rows, cols, feats = queries.shape
    tokens = rows * cols
    per_lat, parts = batch // n_lat, tokens // SUBROWS
    x = jnp.stack([queries, key_vectors, values, upstream]).reshape(4, batch, tokens, feats)
    lat_buf = pltpu.VMEM((4, per_lat, n_lat, tokens, feats), BF16)
    lon_buf = pltpu.VMEM((4, parts, n_lon, SUBROWS, feats), BF16)
    back_buf = pltpu.VMEM((4, batch, tokens, feats), BF16)
    lat_sem = pltpu.SemaphoreType.DMA((per_lat, n_lat))
    lon_sem = pltpu.SemaphoreType.DMA((parts, n_lon))
    y = pl.pallas_call(
        functools.partial(kernel, n_lat, n_lon, cols),
        out_shape=jax.ShapeDtypeStruct((4, batch, tokens, feats), BF16),
        in_specs=[pl.BlockSpec(memory_space=pltpu.VMEM)],
        out_specs=pl.BlockSpec(memory_space=pltpu.VMEM),
        scratch_shapes=[
            lat_buf, lon_buf, lat_buf, lon_buf, back_buf, back_buf,
            lat_sem, lat_sem, lon_sem, lon_sem, lat_sem, lat_sem, lon_sem, lon_sem,
            pltpu.SemaphoreType.DMA((per_lat + parts,)),
        ],
        compiler_params=pltpu.CompilerParams(
            collective_id=0, has_side_effects=True, vmem_limit_bytes=40 * 1024 * 1024
        ),
    )(x)
    return tuple(y[i].reshape(queries.shape) for i in range(4))


def split_heads(tensor):
    leading = tensor.shape[0] * tensor.shape[1]
    return tensor.reshape(leading, tensor.shape[2], tensor.shape[3] // HEAD_DIM, HEAD_DIM)


def lines_whole(items):
    q, k, v, g = (split_heads(item) for item in items)
    dot = functools.partial(jnp.einsum, preferred_element_type=F32)
    probs = jax.nn.softmax(dot("nqhd,nkhd->nhqk", q, k) * SCALE, axis=-1)
    rounded = probs.astype(BF16)
    gprobs = dot("nqhd,nkhd->nhqk", g, v)
    delta = jnp.sum(probs * gprobs, axis=-1, keepdims=True)
    gscores = (probs * (gprobs - delta)).astype(BF16)
    results = (
        dot("nhqk,nkhd->nqhd", rounded, v),
        dot("nhqk,nkhd->nqhd", gscores, k) * SCALE,
        dot("nhqk,nqhd->nkhd", gscores, q) * SCALE,
        dot("nhqk,nqhd->nkhd", rounded, g),
    )
    return tuple(item.astype(BF16).reshape(items[0].shape) for item in results)


def by_exchange(axis, groups, inputs):
    def there(item):
        lines = item.reshape((groups, item.shape[0] * item.shape[1] // groups) + item.shape[2:])
        return lax.all_to_all(lines, axis, split_axis=0, concat_axis=2, tiled=True)

    def back(item):
        item = lax.all_to_all(item, axis, split_axis=2, concat_axis=0, tiled=True)
        return item.reshape(inputs[0].shape)

    return tuple(back(item) for item in lines_whole(tuple(there(item) for item in inputs)))


def by_collectives(n_lat, n_lon, *inputs):
    lon = by_exchange("lon", n_lon, inputs)
    lat = by_exchange("lat", n_lat, tuple(item.transpose(0, 2, 1, 3) for item in inputs))
    return tuple(
        (a.transpose(0, 2, 1, 3).astype(F32) + b.astype(F32)).astype(BF16) for a, b in zip(lat, lon)
    )


def solution(mesh):
    n_lat, n_lon = mesh.shape["lat"], mesh.shape["lon"]

    def on_device(*inputs):
        batch, rows, cols, feats = inputs[0].shape
        fits = (
            batch % n_lat == 0 and batch == n_lon and n_lat > 1 and (rows * cols) % SUBROWS == 0
            and SUBROWS % cols == 0 and feats % LANES == 0 and 2 * HEAD_DIM == LANES
        )
        return (by_kernel if fits else by_collectives)(n_lat, n_lon, *inputs)

    spec = P(None, "lat", "lon", None)
    return jax.shard_map(on_device, mesh=mesh, in_specs=(spec,) * 4, out_specs=(spec,) * 4, check_vma=False)
```

time: 203 us -> 68.7 us (0.34)
  the two profiles are of different devices: /device:TPU:0 before, /device:TPU:9 now
where the time goes in v1:
time: 68.7 us; the launch traced here: 68.5 us
  Pallas kernels  61.9 us (90%)
  local copies, waits for them, and re-layouts  5.68 us (8%)
  between operations  0.71 us (1%)
    pallas_call x1, Pallas kernels, by_kernel(): pl.pallas_call(functools.partial(kernel, n_lat, n_lon, cols), out_shape=j...  61.9 us
    another operation x4, local copies, waits for them, and re-layouts, by_kernel(): return tuple((y[i].reshape(queries.shape) for i in range(4)))  3.21 us
    another operation x4, local copies, waits for them, and re-layouts, by_kernel(): jnp.stack([queries, key_vectors, values, upstream])  2.33 us

profile of v1, /device:TPU:9, one launch (start us, length us, event | category | flops | bytes accessed | tf_op | source)
XLA Modules:
  0.0 68.5 jit_solution(15269008271682646793)
XLA Ops:
  0.6 0.0 copy-start.1
  0.6 0.0 copy-start
  0.7 1.1 %stack.15 = bf16[1,8,32,640]{3,2,1,0:T(8,128)(2,1)S(1)} reshape(bf16[8,8,4,640]{3,2,1,0:T(4,128)(2,1)} %param.4) | data formatting | bytes 655360 | tf_op jit(solution)/shard_map/stack | solution.py:195
  1.8 1.1 %stack.16 = bf16[1,8,32,640]{3,2,1,0:T(8,128)(2,1)S(1)} reshape(bf16[8,8,4,640]{3,2,1,0:T(4,128)(2,1)} %param.5) | data formatting | bytes 655360 | tf_op jit(solution)/shard_map/stack | solution.py:195
  2.8 0.0 copy-done
  2.8 0.1 stack.17
  2.9 0.0 copy-done.1
  2.9 0.1 stack.18
  3.0 0.2 pad_maximum_fusion.x_ref
  3.2 61.9 %shard_map.75 = bf16[4,8,32,640]{3,2,1,0:T(8,128)(2,1)S(1)} custom-call(bf16[4,8,32,640]{3,2,1,0:T(8,128)(2,1)S(1)} %pad_maximum_fusion.x_ref), custom_call_target="tpu_custom_call" | custom-call | tf_op jit(solution)/shard_map/pallas_call | solution.py:201
  65.2 0.1 fusion
  65.3 0.8 %reshape_squeeze.15 = bf16[8,8,4,640]{3,2,1,0:T(4,128)(2,1)} reshape(bf16[1,8,32,640]{3,2,1,0:T(8,128)(2,1)S(1)} %get-tuple-element.4) | data formatting | bytes 655360 | tf_op jit(solution)/shard_map/reshape;squeeze | solution.py:215
  66.1 0.8 %reshape_squeeze.14 = bf16[8,8,4,640]{3,2,1,0:T(4,128)(2,1)} reshape(bf16[1,8,32,640]{3,2,1,0:T(8,128)(2,1)S(1)} %get-tuple-element.5) | data formatting | bytes 655360 | tf_op jit(solution)/shard_map/reshape;squeeze | solution.py:215
  66.9 0.8 %reshape_squeeze.13 = bf16[8,8,4,640]{3,2,1,0:T(4,128)(2,1)} reshape(bf16[1,8,32,640]{3,2,1,0:T(8,128)(2,1)S(1)} %get-tuple-element.6) | data formatting | bytes 655360 | tf_op jit(solution)/shard_map/reshape;squeeze | solution.py:215
  67.7 0.8 %reshape_squeeze.12 = bf16[8,8,4,640]{3,2,1,0:T(4,128)(2,1)} reshape(bf16[1,8,32,640]{3,2,1,0:T(8,128)(2,1)S(1)} %get-tuple-element.7) | data formatting | bytes 655360 | tf_op jit(solution)/shard_map/reshape;squeeze | solution.py:215
Async XLA Ops:
  0.6 2.3 %copy-start.1 = (bf16[8,8,4,640]{3,2,1,0:T(4,128)(2,1)S(1)}, bf16[8,8,4,640]{3,2,1,0:T(4,128)(2,1)}, u32[]{:S(2)}) copy-start(bf16[8,8,4,640]{3,2,1,0:T(4,128)(2,1)} %param.7) | copy-start | bytes 983044
  0.6 2.2 %copy-start = (bf16[8,8,4,640]{3,2,1,0:T(4,128)(2,1)S(1)}, bf16[8,8,4,640]{3,2,1,0:T(4,128)(2,1)}, u32[]{:S(2)}) copy-start(bf16[8,8,4,640]{3,2,1,0:T(4,128)(2,1)} %param.6) | copy-start | bytes 983044

commit v2 on v1

--- a/solution.py
+++ b/solution.py
@@ -45,18 +45,27 @@
 
 
 def kernel(
-    n_lat, n_lon, cols, x_ref, out_ref,
-    in_lat, in_lon, res_lat, res_lon, ret_lat, ret_lon,
-    s_in_lat, r_in_lat, s_in_lon, r_in_lon, s_out_lat, r_out_lat, s_out_lon, r_out_lon, own_sem,
+    n_lat, n_lon, *refs,
 ):
+    given, outs = refs[:4], refs[4:8]
+    (
+        near, x_ref, in_lat, in_lon, res_lat, res_lon, ret_lat, ret_lon,
+    s_in_lat, r_in_lat, s_in_lon, r_in_lon, s_out_lat, r_out_lat, s_out_lon, r_out_lon, own_sem, load_sem,
+    ) = refs[8:]
     me_lat = lax.axis_index("lat")
     me_lon = lax.axis_index("lon")
     _, batch, tokens, feats = x_ref.shape
+    cols = near.shape[3]
+    lines = SUBROWS // cols
     per_lat = batch // n_lat
     parts = tokens // SUBROWS
     lat_peers = [(d, lax.rem(me_lat + d, n_lat)) for d in range(1, n_lat)]
     lon_order = sorted(range(1, n_lon), key=lambda d: abs(d - n_lon // 2))
     lon_peers = [(d, lax.rem(me_lon + d, n_lon)) for d in lon_order]
+
+    loads = [pltpu.make_async_copy(given[a], near.at[a], load_sem.at[a]) for a in range(4)]
+    for copy in loads:
+        copy.start()
 
     barrier = pltpu.get_barrier_semaphore()
     for _, peer in lat_peers:
@@ -95,13 +104,31 @@
             s_out_lon.at[i, d], r_out_lon.at[i, d], {"lon": peer},
         )
 
+    def lay(b, i):
+        for a in range(4):
+            for r in range(lines):
+                x_ref[a, b, pl.ds(i * SUBROWS + r * cols, cols), :] = near[a, b, i * lines + r]
+
+    for copy in loads:
+        copy.wait()
+    for d, peer in lon_peers:
+        lay(peer, 0)
+        lon_in(0, d, peer).start()
+    lay(me_lon, 0)
+
+    def lay_rest(b, carry):
+        for i in range(1, parts):
+            lay(b, i)
+        return carry
+
+    lax.fori_loop(0, batch, lay_rest, 0)
     for i in range(max(per_lat, parts)):
-        if i < parts:
-            for d, peer in lon_peers:
-                lon_in(i, d, peer).start()
         if i < per_lat:
             for d, peer in lat_peers:
                 lat_in(i, d, peer).start()
+        if 0 < i < parts:
+            for d, peer in lon_peers:
+                lon_in(i, d, peer).start()
 
     owns = []
     for i in range(per_lat):
@@ -160,23 +187,24 @@
         keep.start()
         owns[per_lat + i] = keep
 
+    def add(b, i):
+        rows = pl.ds(i * SUBROWS, SUBROWS)
+        for o in range(4):
+            total = ret_lat[o, b, rows, :].astype(F32) + ret_lon[o, b, rows, :].astype(F32)
+            total = total.astype(BF16)
+            for r in range(lines):
+                outs[o][b, i * lines + r] = total[r * cols:(r + 1) * cols]
+
     for copy in owns:
         copy.wait()
     for i in range(per_lat):
         for d, peer in lat_peers:
             lat_out(i, d, peer).wait_recv()
     for i in range(parts):
+        add(me_lon, i)
         for d, peer in lon_peers:
             lon_out(i, d, peer).wait_recv()
-
-        def add(b, carry):
-            rows = pl.ds(i * SUBROWS, SUBROWS)
-            for o in range(4):
-                total = ret_lat[o, b, rows, :].astype(F32) + ret_lon[o, b, rows, :].astype(F32)
-                out_ref[o, b, rows, :] = total.astype(BF16)
-            return carry
-
-        lax.fori_loop(0, batch, add, 0)
+            add(lax.rem(me_lon + n_lon - d, n_lon), i)
 
     for i in range(per_lat):
         for d, peer in lat_peers:
@@ -188,31 +216,51 @@
             lon_out(i, d, peer).wait_send()
 
 
+def store_kernel(*refs):
+    held, outs, sem = refs[:4], refs[4:8], refs[8]
+    copies = [pltpu.make_async_copy(held[o], outs[o], sem.at[o]) for o in range(4)]
+    for copy in copies:
+        copy.start()
+    for copy in copies:
+        copy.wait()
+
+
 def by_kernel(n_lat, n_lon, queries, key_vectors, values, upstream):
     batch, rows, cols, feats = queries.shape
     tokens = rows * cols
     per_lat, parts = batch // n_lat, tokens // SUBROWS
-    x = jnp.stack([queries, key_vectors, values, upstream]).reshape(4, batch, tokens, feats)
     lat_buf = pltpu.VMEM((4, per_lat, n_lat, tokens, feats), BF16)
     lon_buf = pltpu.VMEM((4, parts, n_lon, SUBROWS, feats), BF16)
     back_buf = pltpu.VMEM((4, batch, tokens, feats), BF16)
     lat_sem = pltpu.SemaphoreType.DMA((per_lat, n_lat))
     lon_sem = pltpu.SemaphoreType.DMA((parts, n_lon))
-    y = pl.pallas_call(
-        functools.partial(kernel, n_lat, n_lon, cols),
-        out_shape=jax.ShapeDtypeStruct((4, batch, tokens, feats), BF16),
-        in_specs=[pl.BlockSpec(memory_space=pltpu.VMEM)],
-        out_specs=pl.BlockSpec(memory_space=pltpu.VMEM),
+    queries, key_vectors, values, upstream = (
+        pltpu.with_memory_space_constraint(item, pltpu.HBM) for item in (queries, key_vectors, values, upstream)
+    )
+    held = pl.pallas_call(
+        functools.partial(kernel, n_lat, n_lon),
+        out_shape=(jax.ShapeDtypeStruct(queries.shape, BF16),) * 4,
+        in_specs=[pl.BlockSpec(memory_space=pltpu.HBM)] * 4,
+        out_specs=(pl.BlockSpec(memory_space=pltpu.VMEM),) * 4,
         scratch_shapes=[
+            pltpu.VMEM((4,) + queries.shape, BF16), back_buf,
             lat_buf, lon_buf, lat_buf, lon_buf, back_buf, back_buf,
             lat_sem, lat_sem, lon_sem, lon_sem, lat_sem, lat_sem, lon_sem, lon_sem,
             pltpu.SemaphoreType.DMA((per_lat + parts,)),
+            pltpu.SemaphoreType.DMA((4,)),
         ],
         compiler_params=pltpu.CompilerParams(
             collective_id=0, has_side_effects=True, vmem_limit_bytes=40 * 1024 * 1024
         ),
-    )(x)
-    return tuple(y[i].reshape(queries.shape) for i in range(4))
+    )(queries, key_vectors, values, upstream)
+    return pl.pallas_call(
+        store_kernel,
+        out_shape=(jax.ShapeDtypeStruct(queries.shape, BF16),) * 4,
+        in_specs=[pl.BlockSpec(memory_space=pl.ANY)] * 4,
+        out_specs=(pl.BlockSpec(memory_space=pltpu.HBM),) * 4,
+        scratch_shapes=[pltpu.SemaphoreType.DMA((4,))],
+        compiler_params=pltpu.CompilerParams(vmem_limit_bytes=1024 * 1024),
+    )(*held)
 
 
 def split_heads(tensor):

time: 68.7 us -> 63.7 us (0.927)
  local copies, waits for them, and re-layouts: 5.68 us -> 0 us
  Pallas kernels: 61.9 us -> 62.9 us
    another operation x8 -> x0, local copies, waits for them, and re-layouts: 5.54 us -> none  [the longest x4 3.21 us: by_kernel(): return tuple((y[i].reshape(queries.shape) for i in range(4)))]
    pallas_call x1 -> x2, Pallas kernels: 61.9 us -> 62.9 us  [the longest x1 61.8 us: by_kernel(): pl.pallas_call(functools.partial(kernel, n_lat, n_lon), out_shape=(jax.Sh...]
where the time goes in v2:
time: 63.7 us; the launch traced here: 63.6 us
  Pallas kernels  62.9 us (99%)
  between operations  0.64 us (1%)
    pallas_call x1, Pallas kernels, by_kernel(): pl.pallas_call(functools.partial(kernel, n_lat, n_lon), out_shape=(jax.Sh...  61.8 us

profile of v2, /device:TPU:9, one launch (start us, length us, event | category | flops | bytes accessed | tf_op | source)
XLA Modules:
  0.0 63.6 jit_solution(10355812618127407660)
XLA Ops:
  0.6 61.8 %shard_map.75 = (bf16[8,8,4,640]{3,2,1,0:T(4,128)(2,1)S(1)}, bf16[8,8,4,640]{3,2,1,0:T(4,128)(2,1)S(1)}, bf16[8,8,4,640]{3,2,1,0:T(4,128)(2,1)S(1)}, bf16[8,8,4,640]{3,2,1,0:T(4,128)(2,1)S(1)}) custom-call(bf16[8,8,4,640]{3,2,1,0:T(4,128)(2,1)} %refs_0_.1, bf16[8,8,4,640]{3,2,1,0:T(4,128)(2,1)} %refs_1_.1, bf16[8,8,4,640]{3,2,1,0:T(4,128)(2,1)} %refs_2_.1, ...), custom_call_target="tpu_custom_call" | custom-call | tf_op jit(solution)/shard_map/pallas_call | solution.py:240
  62.5 1.1 %shard_map.76 = (bf16[8,8,4,640]{3,2,1,0:T(4,128)(2,1)}, bf16[8,8,4,640]{3,2,1,0:T(4,128)(2,1)}, bf16[8,8,4,640]{3,2,1,0:T(4,128)(2,1)}, bf16[8,8,4,640]{3,2,1,0:T(4,128)(2,1)}) custom-call(bf16[8,8,4,640]{3,2,1,0:T(4,128)(2,1)S(1)} %get-tuple-element.8.refs_0_, bf16[8,8,4,640]{3,2,1,0:T(4,128)(2,1)S(1)} %get-tuple-element.9.refs_1_, ...), custom_call_target="tpu_custom_call" | custom-call | tf_op jit(solution)/shard_map/pallas_call | solution.py:256

commit v3 on v2

--- a/solution.py
+++ b/solution.py
@@ -60,7 +60,7 @@
     per_lat = batch // n_lat
     parts = tokens // SUBROWS
     lat_peers = [(d, lax.rem(me_lat + d, n_lat)) for d in range(1, n_lat)]
-    lon_order = sorted(range(1, n_lon), key=lambda d: abs(d - n_lon // 2))
+    lon_order = sorted(range(1, n_lon), key=lambda d: (abs(d - n_lon // 2), -d))
     lon_peers = [(d, lax.rem(me_lon + d, n_lon)) for d in lon_order]
 
     loads = [pltpu.make_async_copy(given[a], near.at[a], load_sem.at[a]) for a in range(4)]
@@ -80,10 +80,10 @@
             device_id=target, device_id_type=pl.DeviceIdType.MESH,
         )
 
-    def lat_in(i, d, peer):
+    def lat_in(d, peer):
         return remote(
-            x_ref.at[:, peer * per_lat + i], in_lat.at[:, i, me_lat],
-            s_in_lat.at[i, d], r_in_lat.at[i, d], {"lat": peer},
+            x_ref.at[:, pl.ds(peer * per_lat, per_lat)], in_lat.at[:, :, me_lat],
+            s_in_lat.at[d], r_in_lat.at[d], {"lat": peer},
         )
 
     def lon_in(i, d, peer):
@@ -92,10 +92,10 @@
             s_in_lon.at[i, d], r_in_lon.at[i, d], {"lon": peer},
         )
 
-    def lat_out(i, d, peer):
+    def lat_out(d, peer):
         return remote(
-            res_lat.at[:, i, peer], ret_lat.at[:, me_lat * per_lat + i],
-            s_out_lat.at[i, d], r_out_lat.at[i, d], {"lat": peer},
+            res_lat.at[:, :, peer], ret_lat.at[:, pl.ds(me_lat * per_lat, per_lat)],
+            s_out_lat.at[d], r_out_lat.at[d], {"lat": peer},
         )
 
     def lon_out(i, d, peer):
@@ -122,13 +122,11 @@
         return carry
 
     lax.fori_loop(0, batch, lay_rest, 0)
-    for i in range(max(per_lat, parts)):
-        if i < per_lat:
-            for d, peer in lat_peers:
-                lat_in(i, d, peer).start()
-        if 0 < i < parts:
-            for d, peer in lon_peers:
-                lon_in(i, d, peer).start()
+    for d, peer in lat_peers:
+        lat_in(d, peer).start()
+    for i in range(1, parts):
+        for d, peer in lon_peers:
+            lon_in(i, d, peer).start()
 
     owns = []
     for i in range(per_lat):
@@ -164,17 +162,17 @@
     same_lat = same_line(n_lat * tokens, lambda t: lax.rem(t, cols))
     same_lon = same_line(n_lon * SUBROWS, lambda t: lax.div(lax.rem(t, SUBROWS), cols))
 
+    for d, peer in lat_peers:
+        lat_in(d, peer).wait_recv()
     for i in range(per_lat):
         owns[i].wait()
-        for d, peer in lat_peers:
-            lat_in(i, d, peer).wait_recv()
         attend(in_lat, res_lat, i, same_lat)
-        for d, peer in lat_peers:
-            lat_out(i, d, peer).start()
         keep = pltpu.make_async_copy(
             res_lat.at[:, i, me_lat], ret_lat.at[:, me_lat * per_lat + i], own_sem.at[i])
         keep.start()
         owns[i] = keep
+    for d, peer in lat_peers:
+        lat_out(d, peer).start()
     for i in range(parts):
         owns[per_lat + i].wait()
         for d, peer in lon_peers:
@@ -197,19 +195,17 @@
 
     for copy in owns:
         copy.wait()
-    for i in range(per_lat):
-        for d, peer in lat_peers:
-            lat_out(i, d, peer).wait_recv()
+    for d, peer in lat_peers:
+        lat_out(d, peer).wait_recv()
     for i in range(parts):
         add(me_lon, i)
         for d, peer in lon_peers:
             lon_out(i, d, peer).wait_recv()
             add(lax.rem(me_lon + n_lon - d, n_lon), i)
 
-    for i in range(per_lat):
-        for d, peer in lat_peers:
-            lat_in(i, d, peer).wait_send()
-            lat_out(i, d, peer).wait_send()
+    for d, peer in lat_peers:
+        lat_in(d, peer).wait_send()
+        lat_out(d, peer).wait_send()
     for i in range(parts):
         for d, peer in lon_peers:
             lon_in(i, d, peer).wait_send()
@@ -232,7 +228,7 @@
     lat_buf = pltpu.VMEM((4, per_lat, n_lat, tokens, feats), BF16)
     lon_buf = pltpu.VMEM((4, parts, n_lon, SUBROWS, feats), BF16)
     back_buf = pltpu.VMEM((4, batch, tokens, feats), BF16)
-    lat_sem = pltpu.SemaphoreType.DMA((per_lat, n_lat))
+    lat_sem = pltpu.SemaphoreType.DMA((n_lat,))
     lon_sem = pltpu.SemaphoreType.DMA((parts, n_lon))
     queries, key_vectors, values, upstream = (
         pltpu.with_memory_space_constraint(item, pltpu.HBM) for item in (queries, key_vectors, values, upstream)

time: 63.7 us -> 63.5 us (level)
  no operation moved by 1% of the time
where the time goes in v3:
time: 63.5 us; the launch traced here: 63.3 us
  Pallas kernels  62.7 us (99%)
  between operations  0.64 us (1%)
    pallas_call x1, Pallas kernels, by_kernel(): pl.pallas_call(functools.partial(kernel, n_lat, n_lon), out_shape=(jax.Sh...  61.6 us

profile of v3, /device:TPU:9, one launch (start us, length us, event | category | flops | bytes accessed | tf_op | source)
XLA Modules:
  0.0 63.3 jit_solution(16906228910159481385)
XLA Ops:
  0.6 61.6 %shard_map.75 = (bf16[8,8,4,640]{3,2,1,0:T(4,128)(2,1)S(1)}, bf16[8,8,4,640]{3,2,1,0:T(4,128)(2,1)S(1)}, bf16[8,8,4,640]{3,2,1,0:T(4,128)(2,1)S(1)}, bf16[8,8,4,640]{3,2,1,0:T(4,128)(2,1)S(1)}) custom-call(bf16[8,8,4,640]{3,2,1,0:T(4,128)(2,1)} %refs_0_.1, bf16[8,8,4,640]{3,2,1,0:T(4,128)(2,1)} %refs_1_.1, bf16[8,8,4,640]{3,2,1,0:T(4,128)(2,1)} %refs_2_.1, ...), custom_call_target="tpu_custom_call" | custom-call | tf_op jit(solution)/shard_map/pallas_call | solution.py:236
  62.3 1.1 %shard_map.76 = (bf16[8,8,4,640]{3,2,1,0:T(4,128)(2,1)}, bf16[8,8,4,640]{3,2,1,0:T(4,128)(2,1)}, bf16[8,8,4,640]{3,2,1,0:T(4,128)(2,1)}, bf16[8,8,4,640]{3,2,1,0:T(4,128)(2,1)}) custom-call(bf16[8,8,4,640]{3,2,1,0:T(4,128)(2,1)S(1)} %get-tuple-element.8.refs_0_, bf16[8,8,4,640]{3,2,1,0:T(4,128)(2,1)S(1)} %get-tuple-element.9.refs_1_, ...), custom_call_target="tpu_custom_call" | custom-call | tf_op jit(solution)/shard_map/pallas_call | solution.py:252
